TPU v7x, 256 devices: a whole 4x4x8 slice. The times are simulated.
256 devices in a mesh: patch: 64 (over y, z, core), sample: 4 (over x).
Axes of the slice: x: 4, y: 4, z: 8, core: 2. Of those that a mesh axis runs over, the one named last changes fastest.
Arguments:
- edge_latents: bfloat16 [4, 65536, 512], P('sample', 'patch'), may hold values from -6 to 6
- node_latents: bfloat16 [4, 16384, 512], P('sample', 'patch'), may hold values from -6 to 6
- edge_cotangent: bfloat16 [4, 65536, 512], P('sample', 'patch'), may hold values from -6 to 6
- node_cotangent: bfloat16 [4, 16384, 512], P('sample', 'patch'), may hold values from -6 to 6
- senders: int32 [65536], P('patch'), may hold values from 0 to 575, as said below
- receivers: int32 [65536], P('patch'), may hold values from 0 to 255
- send_rows: int32 [4096, 4], P('patch'), may hold values from 0 to 255
- edge_first: bfloat16 [1536, 512], replicated, may hold values from -0.15625 to 0.15625
- edge_second: bfloat16 [512, 512], replicated, may hold values from -0.25 to 0.25
- edge_gain: float32 [512], replicated, may hold values from 0.25 to 1.75
- node_first: bfloat16 [1024, 512], replicated, may hold values from -0.1875 to 0.1875
- node_second: bfloat16 [512, 512], replicated, may hold values from -0.25 to 0.25
- node_gain: float32 [512], replicated, may hold values from 0.25 to 1.75
Outputs:
- edge_grad: bfloat16 [4, 65536, 512], P('sample', 'patch')
- node_grad: bfloat16 [4, 16384, 512], P('sample', 'patch')
- edge_first_grad: bfloat16 [1536, 512], replicated
- edge_second_grad: bfloat16 [512, 512], replicated
- node_first_grad: bfloat16 [1024, 512], replicated
- node_second_grad: bfloat16 [512, 512], replicated
- edge_gain_grad: bfloat16 [512], replicated
- node_gain_grad: bfloat16 [512], replicated
Inputs may be any that keep to these rules, and one draw needn't show every extreme that they name: `senders`: each patch's sender table has 576 rows: the last 32 nodes of the patch before it (cyclically), its own 256 nodes, the first 32 nodes of the patch after it, then 4 rows from each patch in order.
All inputs are finite; a program needn't handle non-finite values.
Results may differ from a plain program's by a relative error of at most 0.012.
Values may be sent and summed in bfloat16 or wider, within the bound.
A program may use at most 128 MiB of HBM per device.

v0:
```python
import jax
import jax.numpy as jnp
from jax import lax
from jax.sharding import PartitionSpec as P

RIM = 32
FAR = 4


def with_halo(cells, sides, width):
    for axis, dim in sides:
        count = lax.axis_size(axis)
        head = lax.slice_in_dim(cells, 0, width, axis=dim)
        tail = lax.slice_in_dim(cells, cells.shape[dim] - width, cells.shape[dim], axis=dim)
        cells = jnp.concatenate(
            [
                lax.ppermute(tail, axis, [(i, (i + 1) % count) for i in range(count)]),
                cells,
                lax.ppermute(head, axis, [((i + 1) % count, i) for i in range(count)]),
            ],
            axis=dim,
        )
    return cells


def from_behind(array, axis, by):
    size = lax.axis_size(axis)
    return lax.ppermute(array, axis, [(i, (i + by) % size) for i in range(size)])


def normalize(values):
    center = values - jnp.mean(values, axis=1, keepdims=True)
    spread = jnp.mean(center * center, axis=1, keepdims=True)
    scale = lax.rsqrt(spread + 1e-05)
    return (center * scale, scale)


def normalize_back(grads, normed, scale):
    first = jnp.mean(grads, axis=1, keepdims=True)
    second = jnp.mean(grads * normed, axis=1, keepdims=True)
    return (grads - first - normed * second) * scale


def layer_backward(
    edges_in,
    sent_latent,
    nodes_in,
    recv_ids,
    edge_cot,
    node_cot,
    edge_first,
    edge_second,
    edge_gain,
    node_first,
    node_second,
    node_gain,
):
    width = nodes_in.shape[1]
    recv_latent = nodes_in[recv_ids]
    edge_input = jnp.concatenate([edges_in, sent_latent, recv_latent], axis=1)
    edge_pre = jnp.dot(edge_input, edge_first, preferred_element_type=jnp.float32)
    edge_sig = jax.nn.sigmoid(edge_pre)
    edge_act = (edge_pre * edge_sig).astype(jnp.bfloat16)
    edge_raw = jnp.dot(edge_act, edge_second, preferred_element_type=jnp.float32)
    edge_hat, edge_scale = normalize(edge_raw)
    update = edge_hat * edge_gain
    inflow = jax.ops.segment_sum(update, recv_ids, num_segments=nodes_in.shape[0]).astype(
        jnp.bfloat16
    )
    node_input = jnp.concatenate([nodes_in, inflow], axis=1)
    node_pre = jnp.dot(node_input, node_first, preferred_element_type=jnp.float32)
    node_sig = jax.nn.sigmoid(node_pre)
    node_act = (node_pre * node_sig).astype(jnp.bfloat16)
    node_raw = jnp.dot(node_act, node_second, preferred_element_type=jnp.float32)
    node_hat, node_scale = normalize(node_raw)
    node_upstream = node_cot.astype(jnp.float32)
    node_gain_grad = jnp.sum(node_upstream * node_hat, axis=0)
    node_raw_grad = normalize_back(node_upstream * node_gain, node_hat, node_scale).astype(
        jnp.bfloat16
    )
    node_second_grad = jnp.dot(node_act.T, node_raw_grad, preferred_element_type=jnp.float32)
    node_act_grad = jnp.dot(node_raw_grad, node_second.T, preferred_element_type=jnp.float32)
    node_pre_grad = (node_act_grad * node_sig * (1.0 + node_pre * (1.0 - node_sig))).astype(
        jnp.bfloat16
    )
    node_first_grad = jnp.dot(node_input.T, node_pre_grad, preferred_element_type=jnp.float32)
    node_input_grad = jnp.dot(node_pre_grad, node_first.T, preferred_element_type=jnp.float32)
    update_grad = edge_cot.astype(jnp.float32) + node_input_grad[:, width:][recv_ids]
    edge_gain_grad = jnp.sum(update_grad * edge_hat, axis=0)
    edge_raw_grad = normalize_back(update_grad * edge_gain, edge_hat, edge_scale).astype(
        jnp.bfloat16
    )
    edge_second_grad = jnp.dot(edge_act.T, edge_raw_grad, preferred_element_type=jnp.float32)
    edge_act_grad = jnp.dot(edge_raw_grad, edge_second.T, preferred_element_type=jnp.float32)
    edge_pre_grad = (edge_act_grad * edge_sig * (1.0 + edge_pre * (1.0 - edge_sig))).astype(
        jnp.bfloat16
    )
    edge_first_grad = jnp.dot(edge_input.T, edge_pre_grad, preferred_element_type=jnp.float32)
    edge_input_grad = jnp.dot(edge_pre_grad, edge_first.T, preferred_element_type=jnp.float32)
    edge_grad = (edge_cot.astype(jnp.float32) + edge_input_grad[:, :width]).astype(jnp.bfloat16)
    sent_grad = edge_input_grad[:, width : 2 * width]
    node_partial = (
        node_upstream
        + node_input_grad[:, :width]
        + jax.ops.segment_sum(
            edge_input_grad[:, 2 * width :], recv_ids, num_segments=nodes_in.shape[0]
        )
    )
    weight_terms = (
        edge_first_grad,
        edge_second_grad,
        node_first_grad,
        node_second_grad,
        edge_gain_grad,
        node_gain_grad,
    )
    return (edge_grad, sent_grad, node_partial, weight_terms)


def on_device(
    edge_latents,
    node_latents,
    edge_cotangent,
    node_cotangent,
    senders,
    receivers,
    send_rows,
    edge_first,
    edge_second,
    edge_gain,
    node_first,
    node_second,
    node_gain,
):
    patches = lax.axis_size("patch")
    own_nodes = node_latents[0]
    count = own_nodes.shape[0]
    width = own_nodes.shape[1]
    extended = with_halo(own_nodes, (("patch", 0),), RIM)
    outgoing = own_nodes[send_rows]
    incoming = lax.all_to_all(outgoing, "patch", split_axis=0, concat_axis=0, tiled=True)
    table = jnp.concatenate([extended, incoming.reshape(patches * FAR, width)], axis=0)
    edge_grad, sent_grad, node_partial, weight_terms = layer_backward(
        edge_latents[0],
        table[senders],
        own_nodes,
        receivers,
        edge_cotangent[0],
        node_cotangent[0],
        edge_first,
        edge_second,
        edge_gain,
        node_first,
        node_second,
        node_gain,
    )
    table_grad = jax.ops.segment_sum(sent_grad, senders, num_segments=table.shape[0])
    from_next = from_behind(table_grad[:RIM].astype(jnp.bfloat16), "patch", -1).astype(jnp.float32)
    from_prev = from_behind(
        table_grad[RIM + count : 2 * RIM + count].astype(jnp.bfloat16), "patch", 1
    ).astype(jnp.float32)
    far_grad = table_grad[2 * RIM + count :].reshape(patches, FAR, width)
    returned = lax.all_to_all(
        far_grad.astype(jnp.bfloat16), "patch", split_axis=0, concat_axis=0, tiled=True
    ).astype(far_grad.dtype)
    node_total = node_partial + table_grad[RIM : RIM + count]
    node_total = node_total + jnp.pad(from_prev, ((0, count - RIM), (0, 0)))
    node_total = node_total + jnp.pad(from_next, ((count - RIM, 0), (0, 0)))
    node_total = node_total + jax.ops.segment_sum(
        returned.reshape(patches * FAR, width), send_rows.reshape(-1), num_segments=count
    )
    summed = lax.psum(
        (
            weight_terms[0],
            weight_terms[1],
            weight_terms[2],
            weight_terms[3],
            weight_terms[4],
            weight_terms[5],
        ),
        ("patch", "sample"),
    )
    finals = tuple((term.astype(jnp.bfloat16) for term in summed))
    return (
        edge_grad[None],
        node_total.astype(jnp.bfloat16)[None],
        finals[0],
        finals[1],
        finals[2],
        finals[3],
        finals[4],
        finals[5],
    )


def solution(mesh):
    return jax.shard_map(
        on_device,
        mesh=mesh,
        in_specs=(
            P("sample", "patch", None),
            P("sample", "patch", None),
            P("sample", "patch", None),
            P("sample", "patch", None),
            P("patch"),
            P("patch"),
            P("patch", None),
            P(),
            P(),
            P(),
            P(),
            P(),
            P(),
        ),
        out_specs=(
            P("sample", "patch", None),
            P("sample", "patch", None),
            P(),
            P(),
            P(),
            P(),
            P(),
            P(),
        ),
        check_vma=False,
    )
```

profile of v0, /device:TPU:32, one launch (start us, length us, event | category | flops | bytes accessed | tf_op | source)
XLA Modules:
  0.0 275.9 jit_solution(2588927336006680791)
XLA Ops:
  1.7 2.2 gather_fusion
  4.7 11.8 %all-to-all-start = ((bf16[64,4,512]{2,1,0:T(4,128)(2,1)}), bf16[64,4,512]{2,1,0:T(4,128)(2,1)S(1)}, u32[]{:S(2)}, u32[]{:S(2)}) async-start(bf16[64,4,512]{2,1,0:T(4,128)(2,1)} %reshape.83), calls=%async_computation | async-start | bytes 524288 | tf_op jit(solution)/shard_map/all_to_all | solution.py:141
  16.7 1.6 collective-permute-start.1
  19.1 1.5 copy.25
  20.6 5.1 %gather_fusion.2 = bf16[1024,512]{1,0:T(8,128)(2,1)} fusion(bf16[256,512]{1,0:T(8,128)(2,1)S(1)} %bitcast.48, s32[1024]{0:T(1024)S(1)} %fusion.31), kind=kCustom, calls=%fused_computation.2 | custom fusion | bytes 2101248 | tf_op jit(solution)/shard_map/gather | solution.py:59
  25.7 2.8 %all-to-all-done = bf16[64,4,512]{2,1,0:T(4,128)(2,1)S(1)} async-done(((bf16[64,4,512]{2,1,0:T(4,128)(2,1)}), bf16[64,4,512]{2,1,0:T(4,128)(2,1)S(1)}, u32[]{:S(2)}, u32[]{:S(2)}) %all-to-all-start) | async-done | bytes 262176 | tf_op jit(solution)/shard_map/all_to_all | solution.py:141
  30.3 5.1 %gather_fusion.1 = bf16[1024,512]{1,0:T(8,128)(2,1)} fusion(bf16[576,512]{1,0:T(8,128)(2,1)S(1)} %pad_maximum_fusion.3, s32[1024]{0:T(1024)S(1)} %fusion.30), kind=kCustom, calls=%fused_computation.1 | custom fusion | bytes 2101248 | tf_op jit(solution)/shard_map/gather | solution.py:145
  35.3 5.3 %multiply_convert_fusion.2 = (bf16[1024,512]{1,0:T(8,128)(2,1)S(1)}, f32[1024,512]{1,0:T(8,128)}) fusion(bf16[1536,512]{1,0:T(8,128)(2,1)S(1)} %copy-done, bf16[1024,512]{1,0:T(8,128)(2,1)} %gather_fusion.2, bf16[1024,512]{1,0:T(8,128)(2,1)} %gather_fusion.1, bf16[1024,512]{1,0:T(8,128)(2,1)} %bitcast.52), kind=kOutput, calls=%fused_computation.21 | convolution fusion | flops 1622671360 | bytes 7864320 | tf_op jit(solution)/shard_map/dot_general | solution.py:61
  42.7 1.6 fusion.5
  44.3 2.9 %copy.27 = f32[1024,512]{1,0:T(8,128)} copy(f32[1024,512]{0,1:T(8,128)} %fusion.5) | data formatting | bytes 4194304 | tf_op jit(solution)/shard_map/mul | solution.py:66
  47.2 7.6 %scatter_custom_fusion = f32[256,512]{1,0:T(8,128)S(1)} fusion(s32[1024]{0:T(1024)S(1)} %copy-done.18, f32[1024,512]{1,0:T(8,128)} %copy.27, f32[]{:T(128)} %constant.10.clone.1), kind=kCustom, calls=%fused_computation.59 | custom fusion | flops 524288 | bytes 524800 | tf_op jit(solution)/shard_map/scatter-add | solution.py:67
  54.8 1.7 fusion.24
  58.3 1.6 fusion.36
  60.4 1.8 fusion.23
  62.2 4.9 %gather_fusion.3 = f32[1024,512]{1,0:T(8,128)} fusion(f32[256,512]{1,0:T(8,128)S(1)} %slice.63, s32[1024]{0:T(1024)S(1)} %fusion.31), kind=kCustom, calls=%fused_computation.3 | custom fusion | bytes 4198400 | tf_op jit(solution)/shard_map/gather | solution.py:88
  67.1 2.9 %copy.28 = f32[1024,512]{0,1:T(8,128)} copy(f32[1024,512]{1,0:T(8,128)} %gather_fusion.3) | data formatting | bytes 4194304 | tf_op jit(solution)/shard_map/gather | solution.py:88
  70.1 3.2 %multiply_reduce_fusion = (f32[512]{0:T(512)S(1)}, f32[1024]{0:T(1024)S(1)}, f32[1024]{0:T(1024)S(1)}) fusion(f32[1024,512]{0,1:T(8,128)} %copy-done.2, f32[1024]{0:T(1024)S(1)} %add_rsqrt_fusion, f32[1024]{0:T(1024)S(1)} %broadcast_multiply_fusion.2, f32[1024,512]{0,1:T(8,128)} %copy.28, bf16[1,1024,512]{1,2,0:T(8,128)(2,1)S(1)} %copy.25, f32[512]{0:T(512)S(1)} %copy-done.15), kind=kLoop, calls=%fused_computation.16 | loop fusion | flops 5240320 | bytes 5263360 | tf_op jit(solution)/shard_map/reduce_sum | solution.py:89
  74.8 1.7 fusion.45
  76.6 1.3 multiply_convert_fusion
  78.4 3.6 %fusion.6 = f32[1536,512]{1,0:T(8,128)} fusion(bf16[1024,512]{1,0:T(8,128)(2,1)S(1)} %multiply_convert_fusion, bf16[1024,512]{1,0:T(8,128)(2,1)S(1)} %copy-done.7, bf16[1024,512]{1,0:T(8,128)(2,1)S(1)} %copy-done.8, bf16[1024,512]{1,0:T(8,128)(2,1)S(1)} %bitcast.53), kind=kOutput, calls=%fused_computation.26 | convolution fusion | flops 1620049920 | bytes 7340032 | tf_op jit(solution)/shard_map/dot_general | solution.py:98
  82.0 4.5 %fusion.44 = f32[1024,1536]{1,0:T(8,128)} fusion(bf16[1024,512]{1,0:T(8,128)(2,1)S(1)} %multiply_convert_fusion, bf16[1536,512]{1,0:T(8,128)(2,1)S(1)} %copy-done), kind=kOutput, calls=%fused_computation.87 | convolution fusion | flops 1610612736 | bytes 8912896 | tf_op jit(solution)/shard_map/dot_general | solution.py:99
  86.5 8.4 %scatter_custom_fusion.1 = f32[576,512]{1,0:T(8,128)} fusion(s32[1024]{0:T(1024)S(1)} %copy-done.17, f32[1024,1536]{1,0:T(8,128)} %fusion.44, f32[]{:T(128)} %constant.10.clone.1), kind=kCustom, calls=%fused_computation.14 | custom fusion | flops 524288 | bytes 3277312 | tf_op jit(solution)/shard_map/scatter-add | solution.py:157
  94.9 1.3 convert.12
  96.3 3.1 %slice.64 = f32[1024,512]{1,0:T(8,128)} slice(f32[1024,1536]{1,0:T(8,128)} %fusion.44), slice={[0:1024], [0:512]} | slice | bytes 4194304 | tf_op jit(solution)/shard_map/slice | solution.py:100
  100.1 8.7 %all-to-all-start.1 = ((bf16[64,4,512]{2,1,0:T(4,128)(2,1)}), bf16[64,4,512]{2,1,0:T(4,128)(2,1)S(1)}, u32[]{:S(2)}, u32[]{:S(2)}) async-start(bf16[64,4,512]{2,1,0:T(4,128)(2,1)} %convert_element_type.83), calls=%async_computation.1 | async-start | bytes 524288 | tf_op jit(solution)/shard_map/all_to_all | solution.py:163
  109.1 1.6 collective-permute-start.3
  110.7 3.0 %copy.32 = f32[1024,512]{0,1:T(8,128)} copy(f32[1024,512]{1,0:T(8,128)} %slice.64) | data formatting | bytes 4194304
  113.7 144.9 %all-reduce.4 = (bf16[1536,512]{1,0:T(8,128)(2,1)}, bf16[512,512]{1,0:T(8,128)(2,1)}, bf16[1024,512]{1,0:T(8,128)(2,1)}, bf16[512,512]{1,0:T(8,128)(2,1)}, bf16[512]{0:T(512)(128)(2,1)}, /*index=5*/bf16[512]{0:T(512)(128)(2,1)}) all-reduce(f32[1536,512]{1,0:T(8,128)} %fusion.6, ...), channel_id=1, replica_groups=mesh['patch'=64,'sample'=4] {'patch','sample'}, use_global_device_ids=true, to_apply=%region_12.0 | all-reduce | flops 1836032 | bytes 11016192 | tf_op jit(solution)/shard_map/psum | solution.py:172
  258.6 2.9 %fusion.10 = bf16[1,1024,512]{1,2,0:T(8,128)(2,1)} fusion(f32[1024,512]{0,1:T(8,128)} %copy.32, bf16[1,1024,512]{1,2,0:T(8,128)(2,1)S(1)} %copy.25), kind=kLoop, calls=%fused_computation.31 | loop fusion | flops 1572864 | bytes 4194304 | tf_op jit(solution)/shard_map/broadcast_in_dim | solution.py:185
  261.5 2.4 copy.31
  265.1 7.6 %scatter_custom_fusion.2 = f32[256,512]{1,0:T(8,128)S(1)} fusion(f32[256,512]{1,0:T(8,128)S(1)} %fusion.21, s32[1024]{0:T(1024)S(1)} %copy-done.18, f32[1024,1536]{1,0:T(8,128)} %fusion.44), kind=kCustom, calls=%fused_computation.12 | custom fusion | flops 524288 | bytes 2621440 | tf_op jit(solution)/shard_map/scatter-add | solution.py:105
  272.8 2.3 scatter_custom_fusion.3
  (88 shorter events, 14.0 us)
Async XLA Ops:
  0.6 34.7 %copy-start = (bf16[1536,512]{1,0:T(8,128)(2,1)S(1)}, bf16[1536,512]{1,0:T(8,128)(2,1)}, u32[]{:S(2)}) copy-start(bf16[1536,512]{1,0:T(8,128)(2,1)} %param.20) | copy-start | bytes 4718596
  0.6 17.7 %copy-start.16 = (s32[64,4]{0,1:T(4,128)S(1)}, s32[64,4]{0,1:T(4,128)}, u32[]{:S(2)}) copy-start(s32[64,4]{0,1:T(4,128)} %param.19) | copy-start | bytes 3076
  0.7 15.8 %copy-start.1 = (bf16[1,256,512]{2,1,0:T(8,128)(2,1)S(1)}, bf16[1,256,512]{2,1,0:T(8,128)(2,1)}, u32[]{:S(2)}) copy-start(bf16[1,256,512]{2,1,0:T(8,128)(2,1)} %param.14) | copy-start | bytes 786436
  0.7 17.6 %copy-start.18 = (s32[1024]{0:T(1024)S(1)}, s32[1024]{0:T(1024)}, u32[]{:S(2)}) copy-start(s32[1024]{0:T(1024)} %param.18) | copy-start | bytes 12292
  0.7 17.6 %copy-start.17 = (s32[1024]{0:T(1024)S(1)}, s32[1024]{0:T(1024)}, u32[]{:S(2)}) copy-start(s32[1024]{0:T(1024)} %param.17) | copy-start | bytes 12292
  4.7 23.8 %all-to-all-start = ((bf16[64,4,512]{2,1,0:T(4,128)(2,1)}), bf16[64,4,512]{2,1,0:T(4,128)(2,1)S(1)}, u32[]{:S(2)}, u32[]{:S(2)}) async-start(bf16[64,4,512]{2,1,0:T(4,128)(2,1)} %reshape.83), calls=%async_computation | async-start | bytes 524288 | tf_op jit(solution)/shard_map/all_to_all | solution.py:141
  16.5 12.8 %collective-permute-start = (bf16[32,512]{1,0:T(8,128)(2,1)S(1)}, bf16[32,512]{1,0:T(8,128)(2,1)S(1)}, u32[]{:S(2)}, u32[]{:S(2)}) collective-permute-start(bf16[32,512]{1,0:T(8,128)(2,1)S(1)} %get-tuple-element.38), channel_id=1, source_target_pairs={{0,4},{4,8},{8,12},{12,16},{16,20},{20,24},{24,28},{28,32},{32,36}... | collective-permute-start | bytes 98312 | tf_op jit(solution)/shard_map/ppermute | solution.py:17
  16.7 12.6 %collective-permute-start.1 = (bf16[32,512]{1,0:T(8,128)(2,1)S(1)}, bf16[32,512]{1,0:T(8,128)(2,1)S(1)}, u32[]{:S(2)}, u32[]{:S(2)}) collective-permute-start(bf16[32,512]{1,0:T(8,128)(2,1)S(1)} %get-tuple-element.39), channel_id=1, source_target_pairs={{4,0},{8,4},{12,8},{16,12},{20,16},{24,20},{28,24},{32,28},{36,32}... | collective-permute-start | bytes 98312 | tf_op jit(solution)/shard_map/ppermute | solution.py:19
  35.3 5.3 %copy-start.13 = (bf16[512,512]{1,0:T(8,128)(2,1)S(1)}, bf16[512,512]{1,0:T(8,128)(2,1)}, u32[]{:S(2)}) copy-start(bf16[512,512]{1,0:T(8,128)(2,1)} %param.21) | copy-start | bytes 1572868
  40.6 1.1 copy-start.10
  40.6 2.1 copy-start.15
  41.4 1.3 copy-start.2
  54.8 1.8 copy-start.21
  56.5 1.0 copy-start.12
  56.6 0.9 copy-start.19
  58.3 1.6 copy-start.9
  60.4 1.8 copy-start.5
  70.1 3.2 %copy-start.3 = (f32[1024,512]{0,1:T(8,128)S(1)}, f32[1024,512]{0,1:T(8,128)}, u32[]{:S(2)}) copy-start(f32[1024,512]{0,1:T(8,128)} %copy-done.2) | copy-start | bytes 6291460
  70.1 3.5 %copy-start.4 = (f32[1024,512]{0,1:T(8,128)S(1)}, f32[1024,512]{0,1:T(8,128)}, u32[]{:S(2)}) copy-start(f32[1024,512]{0,1:T(8,128)} %copy.28) | copy-start | bytes 6291460
  73.5 1.2 copy-start.11
  74.8 1.8 copy-start.14
  74.8 1.8 copy-start.22
  76.6 1.3 copy-start.7
  76.6 1.5 copy-start.8
  76.6 1.9 copy-start.20
  100.1 172.6 %all-to-all-start.1 = ((bf16[64,4,512]{2,1,0:T(4,128)(2,1)}), bf16[64,4,512]{2,1,0:T(4,128)(2,1)S(1)}, u32[]{:S(2)}, u32[]{:S(2)}) async-start(bf16[64,4,512]{2,1,0:T(4,128)(2,1)} %convert_element_type.83), calls=%async_computation.1 | async-start | bytes 524288 | tf_op jit(solution)/shard_map/all_to_all | solution.py:163
  108.9 155.0 %collective-permute-start.2 = (bf16[32,512]{1,0:T(8,128)(2,1)S(1)}, bf16[32,512]{1,0:T(8,128)(2,1)S(1)}, u32[]{:S(2)}, u32[]{:S(2)}) collective-permute-start(bf16[32,512]{1,0:T(8,128)(2,1)S(1)} %get-tuple-element.36), channel_id=1, source_target_pairs={{0,4},{4,8},{8,12},{12,16},{16,20},{20,24},{24,28},{28,32},{32,36}... | collective-permute-start | bytes 98312 | tf_op jit(solution)/shard_map/ppermute | solution.py:28
  109.1 154.8 %collective-permute-start.3 = (bf16[32,512]{1,0:T(8,128)(2,1)S(1)}, bf16[32,512]{1,0:T(8,128)(2,1)S(1)}, u32[]{:S(2)}, u32[]{:S(2)}) collective-permute-start(bf16[32,512]{1,0:T(8,128)(2,1)S(1)} %get-tuple-element.37), channel_id=1, source_target_pairs={{0,252},{4,0},{8,4},{12,8},{16,12},{20,16},{24,20},{28,24},{32,28}... | collective-permute-start | bytes 98312 | tf_op jit(solution)/shard_map/ppermute | solution.py:28
  261.5 2.4 copy-start.6
where the time goes:
time: 277 us; the launch traced here: 276 us
  blocking collectives  145 us (52%)
  other arithmetic  40.4 us (15%)
  local copies, waits for them, and re-layouts  39 us (14%)
  starting transfers between devices  24.1 us (9%)
  matrix products  23.5 us (8%)
  waiting for transfers between devices  2.85 us (1%)
    psum x1, blocking collectives, on_device(): lax.psum((weight_terms[0], weight_terms[1], weight_terms[2], weight_terms...  145 us
    all_to_all x1, starting transfers between devices, on_device(): lax.all_to_all(outgoing, 'patch', split_axis=0, concat_axis=0, tiled=True)  11.8 us
    unnamed x50, local copies, waits for them, and re-layouts  9.6 us
    all_to_all x1, starting transfers between devices, on_device(): lax.all_to_all(far_grad.astype(jnp.bfloat16), 'patch', split_axis=0, conc...  8.74 us
    scatter-add x1, other arithmetic, on_device(): jax.ops.segment_sum(sent_grad, senders, num_segments=table.shape[0])  8.43 us
    gather x2, local copies, waits for them, and re-layouts, layer_backward(): node_input_grad[:, width:][recv_ids]  7.83 us
    scatter-add x1, other arithmetic, layer_backward(): jax.ops.segment_sum(edge_input_grad[:, 2 * width:], recv_ids, num_segment...  7.62 us
    scatter-add x1, other arithmetic, layer_backward(): jax.ops.segment_sum(update, recv_ids, num_segments=nodes_in.shape[0])  7.56 us
  transfers between devices with their start and end apart: 6, of which 1 were waited for; matrix products, arithmetic and copies ran while one was open for 9% of the time, Pallas kernels for 0%

commit v1 on v0

--- a/solution.py
+++ b/solution.py
@@ -170,15 +170,18 @@
         returned.reshape(patches * FAR, width), send_rows.reshape(-1), num_segments=count
     )
     summed = lax.psum(
-        (
-            weight_terms[0],
-            weight_terms[1],
-            weight_terms[2],
-            weight_terms[3],
-            weight_terms[4],
-            weight_terms[5],
+        lax.psum(
+            (
+                weight_terms[0],
+                weight_terms[1],
+                weight_terms[2],
+                weight_terms[3],
+                weight_terms[4],
+                weight_terms[5],
+            ),
+            "patch",
         ),
-        ("patch", "sample"),
+        "sample",
     )
     finals = tuple((term.astype(jnp.bfloat16) for term in summed))
     return (

time: 277 us -> 435 us (1.57)
  blocking collectives: 145 us -> 257 us
  waiting for transfers between devices: 2.85 us -> 34.8 us
  between operations: 1.02 us -> 14.4 us
    psum x0 -> x1, blocking collectives: none -> 134 us  [on_device(): lax.psum(lax.psum((weight_terms[0], weight_terms[1], weight_terms[2], wei...]
    psum x0 -> x1, waiting for transfers between devices: none -> 31.2 us  [on_device(): lax.psum((weight_terms[0], weight_terms[1], weight_terms[2], weight_terms...]
    psum x1, blocking collectives: 145 us -> 123 us  [on_device(): lax.psum((weight_terms[0], weight_terms[1], weight_terms[2], weight_terms...]
    unnamed x50 -> x56, local copies, waits for them, and re-layouts: 9.6 us -> 10.6 us
  transfers between devices with their start and end apart: 6 -> 7, of which waited for: 1 -> 2; matrix products, arithmetic and copies ran while one was open for 9% -> 11% of each run, Pallas kernels for 0% -> 0%
where the time goes in v1:
time: 435 us; the launch traced here: 434 us
  blocking collectives  257 us (59%)
  local copies, waits for them, and re-layouts  40.2 us (9%)
  other arithmetic  39.3 us (9%)
  waiting for transfers between devices  34.8 us (8%)
  matrix products  24.7 us (6%)
  starting transfers between devices  23.4 us (5%)
  between operations  14.4 us (3%)
    psum x1, blocking collectives, on_device(): lax.psum(lax.psum((weight_terms[0], weight_terms[1], weight_terms[2], wei...  134 us
    psum x1, blocking collectives, on_device(): lax.psum((weight_terms[0], weight_terms[1], weight_terms[2], weight_terms...  123 us
    psum x1, waiting for transfers between devices, on_device(): lax.psum((weight_terms[0], weight_terms[1], weight_terms[2], weight_terms...  31.2 us
    all_to_all x1, starting transfers between devices, on_device(): lax.all_to_all(outgoing, 'patch', split_axis=0, concat_axis=0, tiled=True)  11.8 us
    unnamed x56, local copies, waits for them, and re-layouts  10.6 us
  transfers between devices with their start and end apart: 7, of which 2 were waited for; matrix products, arithmetic and copies ran while one was open for 11% of the time, Pallas kernels for 0%

profile of v1, /device:TPU:32, one launch (start us, length us, event | category | flops | bytes accessed | tf_op | source)
XLA Modules:
  0.0 433.9 jit_solution(17201882210306572581)
XLA Ops:
  8.2 2.2 gather_fusion
  11.2 11.8 %all-to-all-start = ((bf16[64,4,512]{2,1,0:T(4,128)(2,1)}), bf16[64,4,512]{2,1,0:T(4,128)(2,1)S(1)}, u32[]{:S(2)}, u32[]{:S(2)}) async-start(bf16[64,4,512]{2,1,0:T(4,128)(2,1)} %reshape.83), calls=%async_computation | async-start | bytes 524288 | tf_op jit(solution)/shard_map/all_to_all | solution.py:141
  23.3 1.6 collective-permute-start.1
  24.9 1.5 copy.25
  26.4 5.1 %gather_fusion.2 = bf16[1024,512]{1,0:T(8,128)(2,1)} fusion(bf16[256,512]{1,0:T(8,128)(2,1)S(1)} %bitcast.48, s32[1024]{0:T(1024)S(1)} %fusion.31), kind=kCustom, calls=%fused_computation.2 | custom fusion | bytes 2101248 | tf_op jit(solution)/shard_map/gather | solution.py:59
  31.5 3.5 all-to-all-done
  36.8 5.1 %gather_fusion.1 = bf16[1024,512]{1,0:T(8,128)(2,1)} fusion(bf16[576,512]{1,0:T(8,128)(2,1)S(1)} %pad_maximum_fusion.3, s32[1024]{0:T(1024)S(1)} %fusion.30), kind=kCustom, calls=%fused_computation.1 | custom fusion | bytes 2101248 | tf_op jit(solution)/shard_map/gather | solution.py:145
  41.9 5.3 %multiply_convert_fusion.2 = (bf16[1024,512]{1,0:T(8,128)(2,1)S(1)}, f32[1024,512]{1,0:T(8,128)}) fusion(bf16[1536,512]{1,0:T(8,128)(2,1)S(1)} %copy-done, bf16[1024,512]{1,0:T(8,128)(2,1)} %gather_fusion.2, bf16[1024,512]{1,0:T(8,128)(2,1)} %gather_fusion.1, bf16[1024,512]{1,0:T(8,128)(2,1)} %bitcast.52), kind=kOutput, calls=%fused_computation.21 | convolution fusion | flops 1622671360 | bytes 7864320 | tf_op jit(solution)/shard_map/dot_general | solution.py:61
  49.2 1.6 fusion.5
  50.8 2.9 copy.27
  53.7 7.6 %scatter_custom_fusion = f32[256,512]{1,0:T(8,128)S(1)} fusion(s32[1024]{0:T(1024)S(1)} %copy-done.19, f32[1024,512]{1,0:T(8,128)} %copy.27, f32[]{:T(128)} %constant.10.clone.1), kind=kCustom, calls=%fused_computation.59 | custom fusion | flops 524288 | bytes 524800 | tf_op jit(solution)/shard_map/scatter-add | solution.py:67
  61.4 1.7 fusion.24
  64.9 1.5 fusion.36
  66.9 1.8 fusion.23
  68.7 4.9 %gather_fusion.3 = f32[1024,512]{1,0:T(8,128)} fusion(f32[256,512]{1,0:T(8,128)S(1)} %slice.63, s32[1024]{0:T(1024)S(1)} %fusion.31), kind=kCustom, calls=%fused_computation.3 | custom fusion | bytes 4198400 | tf_op jit(solution)/shard_map/gather | solution.py:88
  73.7 2.9 copy.28
  76.6 3.2 multiply_reduce_fusion
  81.3 1.8 fusion.45
  85.4 3.5 fusion.6
  90.3 5.7 %fusion.44 = f32[1024,1536]{1,0:T(8,128)} fusion(bf16[1024,512]{1,0:T(8,128)(2,1)} %copy-done.24, bf16[1536,512]{1,0:T(8,128)(2,1)S(1)} %copy-done), kind=kOutput, calls=%fused_computation.87 | convolution fusion | flops 1610612736 | bytes 8912896 | tf_op jit(solution)/shard_map/dot_general | solution.py:99
  96.0 8.4 %scatter_custom_fusion.1 = f32[576,512]{1,0:T(8,128)} fusion(s32[1024]{0:T(1024)S(1)} %copy-done.18, f32[1024,1536]{1,0:T(8,128)} %fusion.44, f32[]{:T(128)} %constant.10.clone.1), kind=kCustom, calls=%fused_computation.14 | custom fusion | flops 524288 | bytes 3277312 | tf_op jit(solution)/shard_map/scatter-add | solution.py:157
  104.5 3.2 slice.64
  108.6 8.0 %all-to-all-start.1 = ((bf16[64,4,512]{2,1,0:T(4,128)(2,1)}), bf16[64,4,512]{2,1,0:T(4,128)(2,1)S(1)}, u32[]{:S(2)}, u32[]{:S(2)}) async-start(bf16[64,4,512]{2,1,0:T(4,128)(2,1)} %convert_element_type.83), calls=%async_computation.1 | async-start | bytes 524288 | tf_op jit(solution)/shard_map/all_to_all | solution.py:163
  116.8 1.6 collective-permute-start.3
  118.4 2.9 copy.32
  121.3 2.9 fusion.10
  124.3 123.5 %all-reduce.2 = (f32[512]{0:T(512)S(1)}, f32[512]{0:T(512)}) all-reduce(f32[512]{0:T(512)S(1)} %get-tuple-element.24, f32[512]{0:T(512)S(1)} %get-tuple-element.27), channel_id=1, replica_groups=mesh['patch'=64,'sample'=4] {'patch'}, use_global_device_ids=true, to_apply=%region_21.22 | all-reduce | flops 1024 | bytes 8192 | tf_op jit(solution)/shard_map/psum | solution.py:173
  247.7 2.3 copy.31
  251.3 7.7 %scatter_custom_fusion.2 = f32[256,512]{1,0:T(8,128)S(1)} fusion(f32[256,512]{1,0:T(8,128)S(1)} %fusion.21, s32[1024]{0:T(1024)S(1)} %copy-done.19, f32[1024,1536]{1,0:T(8,128)} %fusion.44), kind=kCustom, calls=%fused_computation.12 | custom fusion | flops 524288 | bytes 2621440 | tf_op jit(solution)/shard_map/scatter-add | solution.py:105
  259.0 2.3 scatter_custom_fusion.3
  262.2 31.2 %all-reduce.8.cloned.1.call-done = (f32[1536,512]{1,0:T(8,128)}, f32[512,512]{1,0:T(8,128)}, f32[1024,512]{1,0:T(8,128)}, f32[512,512]{1,0:T(8,128)}) async-done(((f32[1536,512]{1,0:T(8,128)}, f32[512,512]{1,0:T(8,128)}, f32[1024,512]{1,0:T(8,128)}, f32[512,512]{1,0:T(8,128)}), (f32[1536,512]{1,0:T(8,128)}, f32[512,512]{1,0:T(8,128)}, f32[1024,512]{1,0:T(8,128)}, ...) | async-done | bytes 7340048 | tf_op jit(solution)/shard_map/psum | solution.py:173
  293.4 133.6 %all-reduce.9 = (bf16[1536,512]{1,0:T(8,128)(2,1)}, bf16[512,512]{1,0:T(8,128)(2,1)}, bf16[1024,512]{1,0:T(8,128)(2,1)}, bf16[512,512]{1,0:T(8,128)(2,1)}, bf16[512]{0:T(512)(128)(2,1)}, /*index=5*/bf16[512]{0:T(512)(128)(2,1)}) all-reduce(f32[1536,512]{1,0:T(8,128)} %get-tuple-element.32, ...), channel_id=1, replica_groups=mesh['patch'=64,'sample'=4] {'sample'}, use_global_device_ids=true, to_apply=%region_13.14 | all-reduce | flops 1836032 | bytes 11016192 | tf_op jit(solution)/shard_map/psum | solution.py:172
  (98 shorter events, 16.7 us)
Async XLA Ops:
  7.2 34.7 %copy-start = (bf16[1536,512]{1,0:T(8,128)(2,1)S(1)}, bf16[1536,512]{1,0:T(8,128)(2,1)}, u32[]{:S(2)}) copy-start(bf16[1536,512]{1,0:T(8,128)(2,1)} %param.20) | copy-start | bytes 4718596
  7.2 15.9 %copy-start.1 = (bf16[1,256,512]{2,1,0:T(8,128)(2,1)S(1)}, bf16[1,256,512]{2,1,0:T(8,128)(2,1)}, u32[]{:S(2)}) copy-start(bf16[1,256,512]{2,1,0:T(8,128)(2,1)} %param.14) | copy-start | bytes 786436
  7.2 17.7 %copy-start.19 = (s32[1024]{0:T(1024)S(1)}, s32[1024]{0:T(1024)}, u32[]{:S(2)}) copy-start(s32[1024]{0:T(1024)} %param.18) | copy-start | bytes 12292
  7.2 17.7 %copy-start.18 = (s32[1024]{0:T(1024)S(1)}, s32[1024]{0:T(1024)}, u32[]{:S(2)}) copy-start(s32[1024]{0:T(1024)} %param.17) | copy-start | bytes 12292
  11.2 23.8 %all-to-all-start = ((bf16[64,4,512]{2,1,0:T(4,128)(2,1)}), bf16[64,4,512]{2,1,0:T(4,128)(2,1)S(1)}, u32[]{:S(2)}, u32[]{:S(2)}) async-start(bf16[64,4,512]{2,1,0:T(4,128)(2,1)} %reshape.83), calls=%async_computation | async-start | bytes 524288 | tf_op jit(solution)/shard_map/all_to_all | solution.py:141
  23.0 270.4 %all-reduce.8.cloned.1.call-start = ((), (), s32[]{:S(2)}) async-start(), calls=%async_computation.2 | async-start | bytes 14680064 | tf_op jit(solution)/shard_map/psum | solution.py:173
  23.1 12.7 %collective-permute-start = (bf16[32,512]{1,0:T(8,128)(2,1)S(1)}, bf16[32,512]{1,0:T(8,128)(2,1)S(1)}, u32[]{:S(2)}, u32[]{:S(2)}) collective-permute-start(bf16[32,512]{1,0:T(8,128)(2,1)S(1)} %get-tuple-element.44), channel_id=1, source_target_pairs={{0,4},{4,8},{8,12},{12,16},{16,20},{20,24},{24,28},{28,32},{32,36}... | collective-permute-start | bytes 98312 | tf_op jit(solution)/shard_map/ppermute | solution.py:17
  23.3 12.5 %collective-permute-start.1 = (bf16[32,512]{1,0:T(8,128)(2,1)S(1)}, bf16[32,512]{1,0:T(8,128)(2,1)S(1)}, u32[]{:S(2)}, u32[]{:S(2)}) collective-permute-start(bf16[32,512]{1,0:T(8,128)(2,1)S(1)} %get-tuple-element.45), channel_id=1, source_target_pairs={{4,0},{8,4},{12,8},{16,12},{20,16},{24,20},{28,24},{32,28},{36,32}... | collective-permute-start | bytes 98312 | tf_op jit(solution)/shard_map/ppermute | solution.py:19
  41.9 5.3 %copy-start.14 = (bf16[512,512]{1,0:T(8,128)(2,1)S(1)}, bf16[512,512]{1,0:T(8,128)(2,1)}, u32[]{:S(2)}) copy-start(bf16[512,512]{1,0:T(8,128)(2,1)} %param.21) | copy-start | bytes 1572868
  47.1 1.1 copy-start.11
  47.1 2.1 copy-start.16
  47.9 1.3 copy-start.2
  61.3 1.8 copy-start.23
  63.1 1.0 copy-start.13
  63.1 0.9 copy-start.20
  64.8 1.6 copy-start.10
  66.9 1.8 copy-start.6
  76.6 3.2 copy-start.3
  76.6 3.5 copy-start.4
  80.1 1.2 copy-start.12
  81.3 1.8 copy-start.15
  81.3 1.8 copy-start.25
  83.1 2.3 copy-start.8
  83.1 2.3 copy-start.9
  83.1 2.3 copy-start.22
  84.4 1.0 copy-start.24
  104.5 3.2 copy-start.5
  108.6 150.4 %all-to-all-start.1 = ((bf16[64,4,512]{2,1,0:T(4,128)(2,1)}), bf16[64,4,512]{2,1,0:T(4,128)(2,1)S(1)}, u32[]{:S(2)}, u32[]{:S(2)}) async-start(bf16[64,4,512]{2,1,0:T(4,128)(2,1)} %convert_element_type.83), calls=%async_computation.1 | async-start | bytes 524288 | tf_op jit(solution)/shard_map/all_to_all | solution.py:163
  116.6 133.4 %collective-permute-start.2 = (bf16[32,512]{1,0:T(8,128)(2,1)S(1)}, bf16[32,512]{1,0:T(8,128)(2,1)S(1)}, u32[]{:S(2)}, u32[]{:S(2)}) collective-permute-start(bf16[32,512]{1,0:T(8,128)(2,1)S(1)} %get-tuple-element.42), channel_id=1, source_target_pairs={{0,4},{4,8},{8,12},{12,16},{16,20},{20,24},{24,28},{28,32},{32,36}... | collective-permute-start | bytes 98312 | tf_op jit(solution)/shard_map/ppermute | solution.py:28
  116.8 133.2 %collective-permute-start.3 = (bf16[32,512]{1,0:T(8,128)(2,1)S(1)}, bf16[32,512]{1,0:T(8,128)(2,1)S(1)}, u32[]{:S(2)}, u32[]{:S(2)}) collective-permute-start(bf16[32,512]{1,0:T(8,128)(2,1)S(1)} %get-tuple-element.43), channel_id=1, source_target_pairs={{0,252},{4,0},{8,4},{12,8},{16,12},{20,16},{24,20},{28,24},{32,28}... | collective-permute-start | bytes 98312 | tf_op jit(solution)/shard_map/ppermute | solution.py:28
  124.3 125.8 %copy-start.7 = (f32[256,1024]{1,0:T(8,128)S(1)}, f32[256,1024]{1,0:T(8,128)}, u32[]{:S(2)}) copy-start(f32[256,1024]{1,0:T(8,128)} %copy-done.6) | copy-start | bytes 3145732
  251.3 42.1 %copy-start.21 = (f32[512]{0:T(512)S(1)}, f32[512]{0:T(512)}, u32[]{:S(2)}) copy-start(f32[512]{0:T(512)} %get-tuple-element.31) | copy-start | bytes 6148
  (1 other events, 0.7 us)
Sparse Core Ops, SparseCore 0:
  89.0 204.3 all-reduce.7
